TPU v7x, 256 devices: a whole 4x4x8 slice. The times are simulated.
256 devices in a mesh: row: 16 (over z_lo, y, core), col: 16 (over z_hi, x).
Axes of the slice: x: 4, y: 4, z: 8 (z_hi: 4, z_lo: 2; z = z_hi * 2 + z_lo), core: 2. Of those that a mesh axis runs over, the one named last changes fastest.
Arguments:
- source_desc: bfloat16 [32768, 64], P('row', 'col'), may hold values from -9 to 9
- target_desc: bfloat16 [32768, 64], P('col'), may hold values from -9 to 9
- source_mass: bfloat16 [32768], P('row'), may hold values from 0.099609375 to 10
- target_mass: bfloat16 [32768], P('col'), may hold values from 0.099609375 to 10
Outputs:
- cross_source: float32 [32768], P('row')
- cross_target: float32 [32768], P('col')
- self_source: float32 [32768], P('row')
- self_target: float32 [32768], P('col')
All inputs are finite; a program needn't handle non-finite values.
Results may differ from a plain program's by a relative error of at most 0.0003.
Values may be sent and summed in bfloat16 or wider, within the bound.
A program may use at most 64 MiB of HBM per device.

v0:
```python
import math
import jax
import jax.numpy as jnp
from jax import lax
from jax.sharding import PartitionSpec as P

ITERS = 2
EPSILON = 0.25
REACH = 1.0
DAMPING = 1.0 / (1.0 + EPSILON / REACH)


def half_norms(points):
    wide = points.astype(jnp.float32)
    return 0.5 * jnp.sum(wide * wide, axis=1)


def tile_stats(
    left_desc, right_desc, left_norm, right_norm, left_weight, right_weight, want_rows, want_cols
):
    count = left_desc.shape[0]
    block = math.gcd(512, count)
    blocks = count // block
    width = left_desc.shape[1]
    right_count = right_desc.shape[0]
    inputs = (
        left_desc.reshape(blocks, block, width),
        left_norm.reshape(blocks, block),
        left_weight.reshape(blocks, block),
    )

    def advance(carry, pieces):
        piece_desc, piece_norm, piece_weight = pieces
        product = lax.dot_general(
            piece_desc, right_desc, (((1,), (1,)), ((), ())), preferred_element_type=jnp.float32
        )
        scaled = (piece_norm[:, None] + right_norm[None, :] - product) / EPSILON
        emitted = ()
        if want_rows:
            row_score = right_weight[None, :] - scaled
            row_top = jnp.max(row_score, axis=1)
            row_total = jnp.sum(jnp.exp(row_score - row_top[:, None]), axis=1)
            emitted = (row_top, row_total)
        if want_cols:
            col_top, col_total = carry
            col_score = piece_weight[:, None] - scaled
            fresh_top = jnp.maximum(col_top, jnp.max(col_score, axis=0))
            col_total = col_total * jnp.exp(col_top - fresh_top) + jnp.sum(
                jnp.exp(col_score - fresh_top[None, :]), axis=0
            )
            carry = (fresh_top, col_total)
        return (carry, emitted)

    if want_cols:
        start = (
            jnp.full((right_count,), -jnp.inf, jnp.float32),
            jnp.zeros((right_count,), jnp.float32),
        )
    else:
        start = ()
    carry, emitted = lax.scan(advance, start, inputs)
    rows_out = (emitted[0].reshape(count), emitted[1].reshape(count)) if want_rows else None
    cols_out = carry if want_cols else None
    return (rows_out, cols_out)


def reduce_col(maxima, totals):
    merged_top = lax.pmax(maxima, "col")
    merged_total = lax.psum(totals * jnp.exp(maxima - merged_top), "col")
    return merged_top + jnp.log(merged_total)


def reduce_row(maxima, totals):
    merged_top = lax.pmax(maxima, "row")
    merged_total = lax.psum(totals * jnp.exp(maxima - merged_top), "row")
    return merged_top + jnp.log(merged_total)


def body(source_desc, target_desc, source_mass, target_mass):
    row_devices = lax.axis_size("row")
    col_devices = lax.axis_size("col")
    row_index = lax.axis_index("row")
    col_index = lax.axis_index("col")
    tile_count = source_mass.shape[0]
    source_part = tile_count // col_devices
    target_part = target_desc.shape[0] // row_devices
    mass_piece = lax.dynamic_slice_in_dim(source_mass, col_index * source_part, source_part, 0)
    source_rows = lax.all_gather(source_desc, "col", axis=1, tiled=True)
    desc_piece = lax.dynamic_slice_in_dim(source_rows, col_index * source_part, source_part, 0)
    source_cols, source_col_mass = (
        lax.all_gather(desc_piece, "row", axis=0, tiled=True),
        lax.all_gather(mass_piece, "row", axis=0, tiled=True),
    )
    target_piece = lax.dynamic_slice_in_dim(target_desc, row_index * target_part, target_part, 0)
    target_mass_piece = lax.dynamic_slice_in_dim(
        target_mass, row_index * target_part, target_part, 0
    )
    target_rows, target_row_mass = (
        lax.all_gather(target_piece, "col", axis=0, tiled=True),
        lax.all_gather(target_mass_piece, "col", axis=0, tiled=True),
    )
    source_log = jnp.log(source_mass.astype(jnp.float32))
    source_col_log = jnp.log(source_col_mass.astype(jnp.float32))
    target_log = jnp.log(target_mass.astype(jnp.float32))
    target_row_log = jnp.log(target_row_mass.astype(jnp.float32))
    source_row_norm = half_norms(source_rows)
    source_col_norm = half_norms(source_cols)
    target_col_norm = half_norms(target_desc)
    target_row_norm = half_norms(target_rows)
    cross_source = jnp.zeros((tile_count,), jnp.float32)
    cross_target = jnp.zeros((target_desc.shape[0],), jnp.float32)
    self_source = jnp.zeros((tile_count,), jnp.float32)
    self_target = jnp.zeros((target_desc.shape[0],), jnp.float32)
    source_view = jnp.zeros((source_cols.shape[0],), jnp.float32)
    target_view = jnp.zeros((target_rows.shape[0],), jnp.float32)
    for iteration in range(ITERS):
        mirror_work = iteration + 1 < ITERS
        cross_rows, cross_cols = tile_stats(
            source_rows,
            target_desc,
            source_row_norm,
            target_col_norm,
            source_log + cross_source / EPSILON,
            target_log + cross_target / EPSILON,
            True,
            True,
        )
        source_self_rows, source_self_cols = tile_stats(
            source_rows,
            source_cols,
            source_row_norm,
            source_col_norm,
            source_log + self_source / EPSILON,
            source_col_log + source_view / EPSILON,
            True,
            mirror_work,
        )
        target_self_rows, target_self_cols = tile_stats(
            target_rows,
            target_desc,
            target_row_norm,
            target_col_norm,
            target_row_log + target_view / EPSILON,
            target_log + self_target / EPSILON,
            mirror_work,
            True,
        )
        col_maxima = [cross_rows[0], source_self_rows[0]]
        col_totals = [cross_rows[1], source_self_rows[1]]
        row_maxima = [cross_cols[0], target_self_cols[0]]
        row_totals = [cross_cols[1], target_self_cols[1]]
        if mirror_work:
            col_maxima.append(target_self_rows[0])
            col_totals.append(target_self_rows[1])
            row_maxima.append(source_self_cols[0])
            row_totals.append(source_self_cols[1])
        col_logs = reduce_col(jnp.concatenate(col_maxima), jnp.concatenate(col_totals))
        row_logs = reduce_row(jnp.concatenate(row_maxima), jnp.concatenate(row_totals))
        target_count = target_desc.shape[0]
        cross_source = 0.5 * cross_source + 0.5 * DAMPING * (-EPSILON * col_logs[:tile_count])
        self_source = 0.5 * self_source + 0.5 * DAMPING * (
            -EPSILON * col_logs[tile_count : 2 * tile_count]
        )
        cross_target = 0.5 * cross_target + 0.5 * DAMPING * (-EPSILON * row_logs[:target_count])
        self_target = 0.5 * self_target + 0.5 * DAMPING * (
            -EPSILON * row_logs[target_count : 2 * target_count]
        )
        if mirror_work:
            target_view = 0.5 * target_view + 0.5 * DAMPING * (
                -EPSILON * col_logs[2 * tile_count :]
            )
            source_view = 0.5 * source_view + 0.5 * DAMPING * (
                -EPSILON * row_logs[2 * target_count :]
            )
    return (cross_source, cross_target, self_source, self_target)


def solution(mesh):
    return jax.shard_map(
        body,
        mesh=mesh,
        in_specs=(P("row", "col"), P("col", None), P("row"), P("col")),
        out_specs=(P("row"), P("col"), P("row"), P("col")),
        check_vma=False,
    )
```

profile of v0, /device:TPU:32, one launch (start us, length us, event | category | flops | bytes accessed | tf_op | source)
XLA Modules:
  0.0 824.4 jit_solution(18188859646712844108)
XLA Ops:
  0.6 47.2 %all-gather = bf16[16,4,2048]{2,1,0:T(4,128)(2,1)S(1)} all-gather(bf16[1,4,2048]{2,1,0:T(4,128)(2,1)} %bitcast.208), channel_id=1, replica_groups=mesh['row'=16,'col'=16] {'col'}, dimensions={0}, use_global_device_ids=true | all-gather | bytes 278528 | tf_op jit(solution)/shard_map/all_gather | solution.py:88
  47.9 20.2 %all_gather.16 = bf16[2048,64]{0,1:T(8,128)(2,1)S(1)} all-gather(bf16[128,64]{0,1:T(8,128)(2,1)S(1)} %dynamic-slice_bitcast_fusion), channel_id=1, replica_groups=mesh['row'=16,'col'=16] {'row'}, dimensions={0}, use_global_device_ids=true | all-gather | bytes 278528 | tf_op jit(solution)/shard_map/all_gather | solution.py:91
  69.3 16.1 %all-gather.1 = bf16[16,1,128]{2,1,0:T(2,128)(2,1)S(1)} all-gather(bf16[1,1,128]{2,1,0:T(2,128)(2,1)S(1)} %dynamic-slice_bitcast_fusion.2), channel_id=1, replica_groups=mesh['row'=16,'col'=16] {'row'}, dimensions={0}, use_global_device_ids=true | all-gather | bytes 4352 | tf_op jit(solution)/shard_map/all_gather | solution.py:92
  86.6 26.9 %while.95 = (s32[]{:T(128)}, f32[2048]{0:T(1024)S(1)}, f32[2048]{0:T(1024)S(1)}, f32[4,512]{1,0:T(4,128)S(1)}, f32[4,512]{1,0:T(4,128)S(1)}, /*index=5*/f32[4,51...) while((s32[]{:T(128)}, f32[2048]{0:T(1024)S(1)}, ...), condition=%wide.region_14.15_spmd.clone, body=%wide.region_9.14_spmd.clone.sunk | while | flops 147858432 | bytes 9203864 | solution.py:61
  89.8 3.4 exponential_reduce_fusion.18
  96.5 3.4 exponential_reduce_fusion.18
  103.3 3.4 exponential_reduce_fusion.18
  110.0 3.4 exponential_reduce_fusion.18
  113.7 26.7 %while.94 = (s32[]{:T(128)}, f32[2048]{0:T(1024)S(1)}, f32[2048]{0:T(1024)S(1)}, f32[4,512]{1,0:T(4,128)S(1)}, f32[4,512]{1,0:T(4,128)S(1)}, /*index=5*/f32[4,51...) while((s32[]{:T(128)}, f32[2048]{0:T(1024)S(1)}, ...), condition=%wide.region_7.8_spmd.clone, body=%wide.region_2.7_spmd.clone.sunk | while | flops 147858432 | bytes 8941720 | solution.py:61
  136.9 3.4 exponential_reduce_fusion.17
  140.5 39.3 %all_gather.19 = bf16[2048,64]{0,1:T(8,128)(2,1)S(1)} all-gather(bf16[128,64]{0,1:T(8,128)(2,1)S(1)} %constant_dynamic-slice_fusion.11), channel_id=1, replica_groups=mesh['row'=16,'col'=16] {'col'}, dimensions={0}, use_global_device_ids=true | all-gather | bytes 278528 | tf_op jit(solution)/shard_map/all_gather | solution.py:99
  180.3 39.8 %all-gather.2 = bf16[16,1,128]{2,1,0:T(2,128)(2,1)S(1)} all-gather(bf16[1,1,128]{2,1,0:T(2,128)(2,1)S(1)} %dynamic-slice_bitcast_fusion.1), channel_id=1, replica_groups=mesh['row'=16,'col'=16] {'col'}, dimensions={0}, use_global_device_ids=true | all-gather | bytes 4352 | tf_op jit(solution)/shard_map/all_gather | solution.py:100
  220.2 26.7 %while.96 = (s32[]{:T(128)}, f32[2048]{0:T(1024)S(1)}, f32[2048]{0:T(1024)S(1)}, f32[4,512]{1,0:T(4,128)S(1)}, f32[4,512]{1,0:T(4,128)S(1)}, /*index=5*/f32[4,51...) while((s32[]{:T(128)}, f32[2048]{0:T(1024)S(1)}, ...), condition=%wide.region_21.22_spmd.clone, body=%wide.region_16.21_spmd.clone.sunk | while | flops 147858432 | bytes 8941720 | solution.py:61
  246.9 76.7 %pmax.28 = f32[6144]{0:T(1024)S(1)} all-reduce(f32[6144]{0:T(1024)S(1)} %constant_dynamic-update-slice_fusion.8), channel_id=1, replica_groups=mesh['row'=16,'col'=16] {'col'}, use_global_device_ids=true, to_apply=%region_22.23 | all-reduce | flops 6144 | bytes 49152 | tf_op jit(solution)/shard_map/pmax | solution.py:68
  323.7 76.7 %psum.28 = f32[6144]{0:T(1024)S(1)} all-reduce(f32[6144]{0:T(1024)S(1)} %maximum_multiply_fusion), channel_id=1, replica_groups=mesh['row'=16,'col'=16] {'col'}, use_global_device_ids=true, to_apply=%region_23.24 | all-reduce | flops 6144 | bytes 49152 | tf_op jit(solution)/shard_map/psum | solution.py:69
  400.5 22.8 %while.98 = (s32[]{:T(128)}, f32[2048]{0:T(1024)S(1)}, f32[2048]{0:T(1024)S(1)}, f32[4,512]{1,0:T(4,128)S(1)}, f32[4,512]{1,0:T(4,128)S(1)}, /*index=5*/f32[2048...) while((s32[]{:T(128)}, f32[2048]{0:T(1024)S(1)}, ...), condition=%wide.region_41.42_spmd.clone, body=%wide.region_38.0_spmd.clone.sunk | while | flops 141568000 | bytes 8908920 | solution.py:61
  423.3 53.0 %pmax.29 = f32[6144]{0:T(1024)S(1)} all-reduce(f32[6144]{0:T(1024)S(1)} %constant_dynamic-update-slice_fusion.9), channel_id=1, replica_groups=mesh['row'=16,'col'=16] {'row'}, use_global_device_ids=true, to_apply=%region_24.25 | all-reduce | flops 6144 | bytes 49152 | tf_op jit(solution)/shard_map/pmax | solution.py:74
  476.3 53.1 %psum.29 = f32[6144]{0:T(1024)S(1)} all-reduce(f32[6144]{0:T(1024)S(1)} %maximum_multiply_fusion.1), channel_id=1, replica_groups=mesh['row'=16,'col'=16] {'row'}, use_global_device_ids=true, to_apply=%region_25.26 | all-reduce | flops 6144 | bytes 49152 | tf_op jit(solution)/shard_map/psum | solution.py:75
  529.5 26.7 %while.97 = (s32[]{:T(128)}, f32[2048]{0:T(1024)S(1)}, f32[2048]{0:T(1024)S(1)}, f32[4,512]{1,0:T(4,128)S(1)}, f32[4,512]{1,0:T(4,128)S(1)}, /*index=5*/f32[4,51...) while((s32[]{:T(128)}, f32[2048]{0:T(1024)S(1)}, ...), condition=%wide.region_31.32_spmd.clone, body=%wide.region_26.31_spmd.clone.sunk | while | flops 147858432 | bytes 8941720 | solution.py:61
  556.3 52.9 %pmax.31 = f32[4096]{0:T(1024)S(1)} all-reduce(f32[4096]{0:T(1024)S(1)} %constant_dynamic-update-slice_fusion.3), channel_id=1, replica_groups=mesh['row'=16,'col'=16] {'row'}, use_global_device_ids=true, to_apply=%region_42.43 | all-reduce | flops 4096 | bytes 32768 | tf_op jit(solution)/shard_map/pmax | solution.py:74
  609.2 52.9 %psum.31 = f32[4096]{0:T(1024)S(1)} all-reduce(f32[4096]{0:T(1024)S(1)} %maximum_multiply_fusion.3), channel_id=1, replica_groups=mesh['row'=16,'col'=16] {'row'}, use_global_device_ids=true, to_apply=%region_43.44 | all-reduce | flops 4096 | bytes 32768 | tf_op jit(solution)/shard_map/psum | solution.py:75
  662.8 7.4 while.93
  670.3 76.7 %pmax.30 = f32[4096]{0:T(1024)S(1)} all-reduce(f32[4096]{0:T(1024)S(1)} %constant_dynamic-update-slice_fusion.2), channel_id=1, replica_groups=mesh['row'=16,'col'=16] {'col'}, use_global_device_ids=true, to_apply=%region_36.37 | all-reduce | flops 4096 | bytes 32768 | tf_op jit(solution)/shard_map/pmax | solution.py:68
  747.0 76.7 %psum.30 = f32[4096]{0:T(1024)S(1)} all-reduce(f32[4096]{0:T(1024)S(1)} %maximum_multiply_fusion.2), channel_id=1, replica_groups=mesh['row'=16,'col'=16] {'col'}, use_global_device_ids=true, to_apply=%region_37.38 | all-reduce | flops 4096 | bytes 32768 | tf_op jit(solution)/shard_map/psum | solution.py:69
  (251 shorter events, 123.8 us)
Async XLA Ops:
  86.5 27.0 %copy-start = (bf16[2048,64]{0,1:T(8,128)(2,1)S(1)}, bf16[2048,64]{0,1:T(8,128)(2,1)}, u32[]{:S(2)}) copy-start(bf16[2048,64]{0,1:T(8,128)(2,1)} %param.17) | copy-start | bytes 786436
  86.6 27.1 %copy-start.1 = (bf16[2048]{0:T(1024)(128)(2,1)S(1)}, bf16[2048]{0:T(1024)(128)(2,1)}, u32[]{:S(2)}) copy-start(bf16[2048]{0:T(1024)(128)(2,1)} %param.19) | copy-start | bytes 12292
  220.2 180.3 %copy-start.2 = (bf16[2048]{0:T(1024)(128)(2,1)S(1)}, bf16[2048]{0:T(1024)(128)(2,1)}, u32[]{:S(2)}) copy-start(bf16[2048]{0:T(1024)(128)(2,1)} %param.18) | copy-start | bytes 12292
where the time goes:
time: 825 us; the launch traced here: 824 us
  blocking collectives  682 us (83%)
  other arithmetic  70.6 us (9%)
  matrix products  65.9 us (8%)
    pmax x2, blocking collectives, reduce_col(): merged_top = lax.pmax(maxima, 'col')  153 us
    psum x2, blocking collectives, reduce_col(): merged_total = lax.psum(totals * jnp.exp(maxima - merged_top), 'col')  153 us
    psum x2, blocking collectives, reduce_row(): merged_total = lax.psum(totals * jnp.exp(maxima - merged_top), 'row')  106 us
    pmax x2, blocking collectives, reduce_row(): merged_top = lax.pmax(maxima, 'row')  106 us
    dot_general x24, matrix products, advance(): lax.dot_general(piece_desc, right_desc, (((1,), (1,)), ((), ())), preferr...  65.9 us
    reduce_sum x20, other arithmetic, advance(): row_total = jnp.sum(jnp.exp(row_score - row_top[:, None]), axis=1)  56.8 us
    all_gather x1, blocking collectives, body(): source_rows = lax.all_gather(source_desc, 'col', axis=1, tiled=True)  47.2 us
    all_gather x1, blocking collectives, body(): lax.all_gather(target_mass_piece, 'col', axis=0, tiled=True)  39.8 us

commit v1 on v0

--- a/solution.py
+++ b/solution.py
@@ -72,7 +72,7 @@
 
 def reduce_row(maxima, totals):
     merged_top = lax.pmax(maxima, "row")
-    merged_total = lax.psum(totals * jnp.exp(maxima - merged_top), "row")
+    merged_total = jnp.sum(lax.all_gather(totals * jnp.exp(maxima - merged_top), "row"), axis=0)
     return merged_top + jnp.log(merged_total)
 
 

time: 825 us -> 756 us (0.916)
  blocking collectives: 682 us -> 611 us
    psum x2 -> x0, blocking collectives: 106 us -> none  [reduce_row(): merged_total = lax.psum(totals * jnp.exp(maxima - merged_top), 'row')]
    all_gather x0 -> x2, blocking collectives: none -> 33.9 us  [reduce_row(): lax.all_gather(totals * jnp.exp(maxima - merged_top), 'row')]
where the time goes in v1:
time: 756 us; the launch traced here: 754 us
  blocking collectives  611 us (81%)
  other arithmetic  70.8 us (9%)
  matrix products  66.1 us (9%)
    pmax x2, blocking collectives, reduce_col(): merged_top = lax.pmax(maxima, 'col')  153 us
    psum x2, blocking collectives, reduce_col(): merged_total = lax.psum(totals * jnp.exp(maxima - merged_top), 'col')  153 us
    pmax x2, blocking collectives, reduce_row(): merged_top = lax.pmax(maxima, 'row')  108 us
    dot_general x24, matrix products, advance(): lax.dot_general(piece_desc, right_desc, (((1,), (1,)), ((), ())), preferr...  66.1 us
    reduce_sum x20, other arithmetic, advance(): row_total = jnp.sum(jnp.exp(row_score - row_top[:, None]), axis=1)  56.8 us
    all_gather x1, blocking collectives, body(): source_rows = lax.all_gather(source_desc, 'col', axis=1, tiled=True)  47.2 us
    all_gather x1, blocking collectives, body(): lax.all_gather(target_mass_piece, 'col', axis=0, tiled=True)  39.8 us
    all_gather x1, blocking collectives, body(): lax.all_gather(target_piece, 'col', axis=0, tiled=True)  39.3 us

profile of v1, /device:TPU:32, one launch (start us, length us, event | category | flops | bytes accessed | tf_op | source)
XLA Modules:
  0.0 754.5 jit_solution(1799257925833417564)
XLA Ops:
  0.6 47.2 %all-gather.2 = bf16[16,4,2048]{2,1,0:T(4,128)(2,1)S(1)} all-gather(bf16[1,4,2048]{2,1,0:T(4,128)(2,1)} %bitcast.208), channel_id=1, replica_groups=mesh['row'=16,'col'=16] {'col'}, dimensions={0}, use_global_device_ids=true | all-gather | bytes 278528 | tf_op jit(solution)/shard_map/all_gather | solution.py:88
  47.9 20.2 %all_gather.28 = bf16[2048,64]{0,1:T(8,128)(2,1)S(1)} all-gather(bf16[128,64]{0,1:T(8,128)(2,1)S(1)} %dynamic-slice_bitcast_fusion), channel_id=1, replica_groups=mesh['row'=16,'col'=16] {'row'}, dimensions={0}, use_global_device_ids=true | all-gather | bytes 278528 | tf_op jit(solution)/shard_map/all_gather | solution.py:91
  69.3 16.1 %all-gather.3 = bf16[16,1,128]{2,1,0:T(2,128)(2,1)S(1)} all-gather(bf16[1,1,128]{2,1,0:T(2,128)(2,1)S(1)} %dynamic-slice_bitcast_fusion.2), channel_id=1, replica_groups=mesh['row'=16,'col'=16] {'row'}, dimensions={0}, use_global_device_ids=true | all-gather | bytes 4352 | tf_op jit(solution)/shard_map/all_gather | solution.py:92
  86.6 27.0 %while.95 = (s32[]{:T(128)}, f32[2048]{0:T(1024)S(1)}, f32[2048]{0:T(1024)S(1)}, f32[4,512]{1,0:T(4,128)S(1)}, f32[4,512]{1,0:T(4,128)S(1)}, /*index=5*/f32[4,51...) while((s32[]{:T(128)}, f32[2048]{0:T(1024)S(1)}, ...), condition=%wide.region_14.15_spmd.clone, body=%wide.region_9.14_spmd.clone.sunk | while | flops 147858432 | bytes 9203864 | solution.py:61
  89.8 3.4 exponential_reduce_fusion.18
  113.7 26.8 %while.94 = (s32[]{:T(128)}, f32[2048]{0:T(1024)S(1)}, f32[2048]{0:T(1024)S(1)}, f32[4,512]{1,0:T(4,128)S(1)}, f32[4,512]{1,0:T(4,128)S(1)}, /*index=5*/f32[4,51...) while((s32[]{:T(128)}, f32[2048]{0:T(1024)S(1)}, ...), condition=%wide.region_7.8_spmd.clone, body=%wide.region_2.7_spmd.clone.sunk | while | flops 147858432 | bytes 8941720 | solution.py:61
  140.5 39.3 %all_gather.31 = bf16[2048,64]{0,1:T(8,128)(2,1)S(1)} all-gather(bf16[128,64]{0,1:T(8,128)(2,1)S(1)} %constant_dynamic-slice_fusion.11), channel_id=1, replica_groups=mesh['row'=16,'col'=16] {'col'}, dimensions={0}, use_global_device_ids=true | all-gather | bytes 278528 | tf_op jit(solution)/shard_map/all_gather | solution.py:99
  180.4 39.8 %all-gather.4 = bf16[16,1,128]{2,1,0:T(2,128)(2,1)S(1)} all-gather(bf16[1,1,128]{2,1,0:T(2,128)(2,1)S(1)} %dynamic-slice_bitcast_fusion.1), channel_id=1, replica_groups=mesh['row'=16,'col'=16] {'col'}, dimensions={0}, use_global_device_ids=true | all-gather | bytes 4352 | tf_op jit(solution)/shard_map/all_gather | solution.py:100
  220.2 26.8 %while.96 = (s32[]{:T(128)}, f32[2048]{0:T(1024)S(1)}, f32[2048]{0:T(1024)S(1)}, f32[4,512]{1,0:T(4,128)S(1)}, f32[4,512]{1,0:T(4,128)S(1)}, /*index=5*/f32[4,51...) while((s32[]{:T(128)}, f32[2048]{0:T(1024)S(1)}, ...), condition=%wide.region_21.22_spmd.clone, body=%wide.region_16.21_spmd.clone.sunk | while | flops 147858432 | bytes 8941720 | solution.py:61
  247.0 76.7 %pmax.28 = f32[6144]{0:T(1024)S(1)} all-reduce(f32[6144]{0:T(1024)S(1)} %constant_dynamic-update-slice_fusion.8), channel_id=1, replica_groups=mesh['row'=16,'col'=16] {'col'}, use_global_device_ids=true, to_apply=%region_22.23 | all-reduce | flops 6144 | bytes 49152 | tf_op jit(solution)/shard_map/pmax | solution.py:68
  323.8 76.7 %psum.14 = f32[6144]{0:T(1024)S(1)} all-reduce(f32[6144]{0:T(1024)S(1)} %maximum_multiply_fusion), channel_id=1, replica_groups=mesh['row'=16,'col'=16] {'col'}, use_global_device_ids=true, to_apply=%region_23.24 | all-reduce | flops 6144 | bytes 49152 | tf_op jit(solution)/shard_map/psum | solution.py:69
  400.6 22.8 %while.98 = (s32[]{:T(128)}, f32[2048]{0:T(1024)S(1)}, f32[2048]{0:T(1024)S(1)}, f32[4,512]{1,0:T(4,128)S(1)}, f32[4,512]{1,0:T(4,128)S(1)}, /*index=5*/f32[2048...) while((s32[]{:T(128)}, f32[2048]{0:T(1024)S(1)}, ...), condition=%wide.region_41.42_spmd.clone, body=%wide.region_38.0_spmd.clone.sunk | while | flops 141568000 | bytes 8908920 | solution.py:61
  423.4 53.0 %pmax.29 = f32[6144]{0:T(1024)S(1)} all-reduce(f32[6144]{0:T(1024)S(1)} %constant_dynamic-update-slice_fusion.9), channel_id=1, replica_groups=mesh['row'=16,'col'=16] {'row'}, use_global_device_ids=true, to_apply=%region_24.25 | all-reduce | flops 6144 | bytes 49152 | tf_op jit(solution)/shard_map/pmax | solution.py:74
  476.4 17.3 %all-gather = f32[98304]{0:T(1024)S(1)} all-gather(f32[6144]{0:T(1024)S(1)} %maximum_multiply_fusion.1), channel_id=2, replica_groups=mesh['row'=16,'col'=16] {'row'}, dimensions={0}, use_global_device_ids=true | all-gather | bytes 417792 | tf_op jit(solution)/shard_map/all_gather | solution.py:75
  493.9 26.8 %while.97 = (s32[]{:T(128)}, f32[2048]{0:T(1024)S(1)}, f32[2048]{0:T(1024)S(1)}, f32[4,512]{1,0:T(4,128)S(1)}, f32[4,512]{1,0:T(4,128)S(1)}, /*index=5*/f32[4,51...) while((s32[]{:T(128)}, f32[2048]{0:T(1024)S(1)}, ...), condition=%wide.region_31.32_spmd.clone, body=%wide.region_26.31_spmd.clone.sunk | while | flops 147858432 | bytes 8941720 | solution.py:61
  497.1 3.4 exponential_reduce_fusion.20
  503.8 3.4 exponential_reduce_fusion.20
  510.5 3.4 exponential_reduce_fusion.20
  517.2 3.4 exponential_reduce_fusion.20
  520.8 54.7 %pmax.31 = f32[4096]{0:T(1024)S(1)} all-reduce(f32[4096]{0:T(1024)S(1)} %constant_dynamic-update-slice_fusion.3), channel_id=1, replica_groups=mesh['row'=16,'col'=16] {'row'}, use_global_device_ids=true, to_apply=%region_42.43 | all-reduce | flops 4096 | bytes 32768 | tf_op jit(solution)/shard_map/pmax | solution.py:74
  575.5 16.7 %all-gather.1 = f32[65536]{0:T(1024)S(1)} all-gather(f32[4096]{0:T(1024)S(1)} %maximum_multiply_fusion.3), channel_id=3, replica_groups=mesh['row'=16,'col'=16] {'row'}, dimensions={0}, use_global_device_ids=true | all-gather | bytes 278528 | tf_op jit(solution)/shard_map/all_gather | solution.py:75
  592.9 7.5 while.93
  600.4 76.7 %pmax.30 = f32[4096]{0:T(1024)S(1)} all-reduce(f32[4096]{0:T(1024)S(1)} %constant_dynamic-update-slice_fusion.2), channel_id=1, replica_groups=mesh['row'=16,'col'=16] {'col'}, use_global_device_ids=true, to_apply=%region_36.37 | all-reduce | flops 4096 | bytes 32768 | tf_op jit(solution)/shard_map/pmax | solution.py:68
  677.1 76.7 %psum.15 = f32[4096]{0:T(1024)S(1)} all-reduce(f32[4096]{0:T(1024)S(1)} %maximum_multiply_fusion.2), channel_id=1, replica_groups=mesh['row'=16,'col'=16] {'col'}, use_global_device_ids=true, to_apply=%region_37.38 | all-reduce | flops 4096 | bytes 32768 | tf_op jit(solution)/shard_map/psum | solution.py:69
  (255 shorter events, 124.3 us)
Async XLA Ops:
  86.5 27.0 %copy-start = (bf16[2048,64]{0,1:T(8,128)(2,1)S(1)}, bf16[2048,64]{0,1:T(8,128)(2,1)}, u32[]{:S(2)}) copy-start(bf16[2048,64]{0,1:T(8,128)(2,1)} %param.17) | copy-start | bytes 786436
  86.6 27.1 %copy-start.1 = (bf16[2048]{0:T(1024)(128)(2,1)S(1)}, bf16[2048]{0:T(1024)(128)(2,1)}, u32[]{:S(2)}) copy-start(bf16[2048]{0:T(1024)(128)(2,1)} %param.19) | copy-start | bytes 12292
  220.2 180.3 %copy-start.2 = (bf16[2048]{0:T(1024)(128)(2,1)S(1)}, bf16[2048]{0:T(1024)(128)(2,1)}, u32[]{:S(2)}) copy-start(bf16[2048]{0:T(1024)(128)(2,1)} %param.18) | copy-start | bytes 12292
